TPU v7x, 256 devices: a whole 4x4x8 slice. The times are simulated.
256 devices in a mesh: rows: 64 (over y_lo, z, x), cols: 4 (over y_hi, core).
Axes of the slice: x: 4, y: 4 (y_hi: 2, y_lo: 2; y = y_hi * 2 + y_lo), z: 8, core: 2. Of those that a mesh axis runs over, the one named last changes fastest.
Arguments:
- inputs: bfloat16 [2, 256, 512, 512], P(None, 'rows', 'cols'), may hold values from -6 to 6
- tight_conv_kernel: bfloat16 [3, 3, 512, 512], P(None, None, 'rows'), may hold values from -0.09375 to 0.09375
- wide_conv_kernel: bfloat16 [3, 3, 512, 512], P(None, None, 'rows'), may hold values from -0.09375 to 0.09375
- up_weight: bfloat16 [512, 2048], P(None, 'rows'), may hold values from -0.25 to 0.25
- down_weight: bfloat16 [2048, 512], P('rows'), may hold values from -0.125 to 0.125
Outputs:
- outputs: bfloat16 [2, 256, 512, 512], P(None, 'rows', 'cols')
All inputs are finite; a program needn't handle non-finite values.
Results may differ from a plain program's by a relative error of at most 0.007.
Values may be sent and summed in bfloat16 or wider, within the bound.
No kernel may reach another device: no remote copies, remote signals or barrier semaphores. Data moves between devices by JAX's collectives and lax.ppermute only.
A program may use at most 64 MiB of HBM per device.

v0:
```python
import jax
import jax.numpy as jnp
from jax import lax
from jax.sharding import PartitionSpec as P

TIGHT_DILATION = 16
WIDE_DILATION = 64


def extended(cells, sides, width):
    for axis, dim in sides:
        count = lax.axis_size(axis)
        ends = count - 1
        head = lax.slice_in_dim(cells, 0, width, axis=dim)
        tail = lax.slice_in_dim(cells, cells.shape[dim] - width, cells.shape[dim], axis=dim)
        cells = jnp.concatenate(
            [
                lax.ppermute(tail, axis, [(i, (i + 1) % count) for i in range(ends)]),
                cells,
                lax.ppermute(head, axis, [((i + 1) % count, i) for i in range(ends)]),
            ],
            axis=dim,
        )
    return cells


def passed_along(array, axis, by):
    devices = lax.axis_size(axis)
    pairs = [(i, i + by) for i in range(devices) if 0 <= i + by < devices]
    return lax.ppermute(array, axis, pairs)


def rms_normalize(values):
    widened = values.astype(jnp.float32)
    scaled = widened * lax.rsqrt(jnp.mean(widened * widened, axis=-1, keepdims=True) + 1e-06)
    return scaled.astype(jnp.bfloat16)


def row_tap(source, offset, mover):
    row_count = source.shape[1]
    if offset >= 0:
        steps_over, remain = divmod(offset, row_count)
        nearer = mover(source, -steps_over)
        return nearer
    steps_over, remain = divmod(-offset, row_count)
    later_rows = mover(source, steps_over)
    return later_rows


def apply_convolution(normed, weight, spread, far_reach):
    col_count = normed.shape[2]
    channel_count = normed.shape[3]
    if far_reach:
        widened = extended(normed, (("cols", 2),), spread)

        def mover(source, by):
            return passed_along(source, "rows", by)

    else:
        widened = extended(normed, (("cols", 2),), spread)

        def mover(source, by):
            return passed_along(source, "rows", by)

    taps = [row_tap(widened, -spread, mover), widened, row_tap(widened, spread, mover)]
    windows = []
    for row_index in range(3):
        for col_index in range(3):
            window = taps[row_index][:, :, col_index * spread : col_index * spread + col_count]
            windows.append(window.reshape(-1, channel_count))
    zeroed = jnp.zeros((windows[0].shape[0], weight.shape[3]), jnp.float32)

    def add_taps(summed, piece):
        for tap_index in range(9):
            row_index, col_index = divmod(tap_index, 3)
            part = windows[tap_index]
            summed = summed + jnp.dot(
                part, piece[row_index, col_index], preferred_element_type=jnp.float32
            )
        return summed

    if far_reach:
        summed = add_taps(zeroed, lax.all_gather(weight, "rows", axis=2, tiled=True))
    else:
        summed = add_taps(zeroed, lax.all_gather(weight, "rows", axis=2, tiled=True))
    return summed.reshape(normed.shape)


def make_adder(features, pieces):
    up_piece, down_piece = pieces
    product = lax.dot_general(
        features, up_piece, (((1,), (1,)), ((), ())), preferred_element_type=jnp.float32
    )
    hidden = jax.nn.gelu(product).astype(jnp.bfloat16)
    return jnp.dot(hidden, down_piece, preferred_element_type=jnp.float32)


def feed_forward(normed_rows, up_weight, down_weight):
    up_rows = up_weight.T
    return make_adder(
        normed_rows,
        (
            lax.all_gather(up_rows, "rows", axis=0, tiled=True),
            lax.all_gather(down_weight, "rows", axis=0, tiled=True),
        ),
    )


def shards(inputs, tight_conv_kernel, wide_conv_kernel, up_weight, down_weight):
    tight_conv_result = (
        inputs.astype(jnp.float32)
        + apply_convolution(rms_normalize(inputs), tight_conv_kernel, TIGHT_DILATION, False)
    ).astype(jnp.bfloat16)
    wide_conv_result = (
        tight_conv_result.astype(jnp.float32)
        + apply_convolution(rms_normalize(tight_conv_result), wide_conv_kernel, WIDE_DILATION, True)
    ).astype(jnp.bfloat16)
    mlp_rows = rms_normalize(wide_conv_result).reshape(-1, wide_conv_result.shape[3])
    branch = feed_forward(mlp_rows, up_weight, down_weight)
    return (wide_conv_result.astype(jnp.float32) + branch.reshape(wide_conv_result.shape)).astype(
        jnp.bfloat16
    )


def solution(mesh):
    placed = (
        P(None, "rows", "cols", None),
        P(None, None, "rows", None),
        P(None, None, "rows", None),
        P(None, "rows"),
        P("rows", None),
    )
    return jax.shard_map(
        shards, mesh=mesh, in_specs=placed, out_specs=P(None, "rows", "cols", None), check_vma=False
    )
```

profile of v0, /device:TPU:16, one launch (start us, length us, event | category | flops | bytes accessed | tf_op | source)
XLA Modules:
  0.0 1360.5 jit_solution(9043071128753244014)
XLA Ops:
  11.1 1.9 collective-permute-start
  13.1 5.1 collective-permute-start.1
  18.9 1.8 collective-permute-done.1
  23.2 4.6 collective-permute-start.2
  27.9 2.1 pad_maximum_fusion.5
  30.0 27.6 %collective-permute-done.3 = bf16[2,4,160,512]{3,2,1,0:T(8,128)(2,1)} collective-permute-done((bf16[2,4,160,512]{3,2,1,0:T(8,128)(2,1)}, bf16[2,4,160,512]{3,2,1,0:T(8,128)(2,1)}, u32[]{:S(2)}, u32[]{:S(2)}) %collective-permute-start.3) | collective-permute-done | bytes 1310752 | tf_op jit(solution)/shard_map/ppermute | solution.py:30
  57.6 3.8 fusion.47
  61.4 1.8 fusion.48
  63.3 253.5 %all-gather.5.cloned.1.call-done = bf16[3,3,512,512]{3,2,1,0:T(8,128)(2,1)} async-done(((bf16[3,3,8,512]{3,2,1,0:T(8,128)(2,1)}), bf16[3,3,512,512]{3,2,1,0:T(8,128)(2,1)}) %all-gather.5.cloned.1.call-update) | async-done | bytes 4718608 | tf_op jit(solution)/shard_map/all_gather | solution.py:85
  316.7 2.2 fusion.31
  319.0 1.8 fusion.32
  328.6 1.9 collective-permute-start.4
  330.6 5.1 collective-permute-start.5
  335.7 6.6 collective-permute-done.4
  342.3 1.6 collective-permute-done.5
  346.7 9.9 collective-permute-start.6
  356.6 344.9 %all-gather.7.cloned.1.call-done = bf16[3,3,512,512]{3,2,1,0:T(8,128)(2,1)} async-done(((bf16[3,3,8,512]{3,2,1,0:T(8,128)(2,1)}), bf16[3,3,512,512]{3,2,1,0:T(8,128)(2,1)}) %all-gather.7.cloned.1.call-update) | async-done | bytes 4718608 | tf_op jit(solution)/shard_map/all_gather | solution.py:83
  701.5 1.9 fusion.25
  705.5 2.1 fusion.45
  709.0 2.2 fusion.46
  715.2 328.8 %all-gather.11.cloned.1.call-done = bf16[2048,512]{1,0:T(8,128)(2,1)} async-done(((bf16[32,512]{1,0:T(8,128)(2,1)}), bf16[2048,512]{1,0:T(8,128)(2,1)}) %all-gather.11.cloned.1.call-update) | async-done | bytes 2097168 | tf_op jit(solution)/shard_map/all_gather | solution.py:104
  1044.0 298.9 %all-gather.9.cloned.1.call-done = bf16[2048,512]{1,0:T(8,128)(2,1)} async-done(((bf16[32,512]{1,0:T(8,128)(2,1)}), bf16[2048,512]{1,0:T(8,128)(2,1)}) %all-gather.9.cloned.1.call-update) | async-done | bytes 2097168 | tf_op jit(solution)/shard_map/all_gather | solution.py:103
  1342.9 8.2 fusion.8
  1351.0 2.9 fusion.18
  (63 shorter events, 25.7 us)
Async XLA Ops:
  6.5 310.2 %all-gather.5.cloned.1.call-start = ((), (), s32[]{:S(2)}) async-start(), calls=%async_computation | async-start | bytes 4792320 | tf_op jit(solution)/shard_map/all_gather | solution.py:85
  7.3 694.3 %all-gather.7.cloned.1.call-start = ((), (), s32[]{:S(2)}) async-start(), calls=%async_computation.1 | async-start | bytes 4792320 | tf_op jit(solution)/shard_map/all_gather | solution.py:83
  8.0 1036.0 %all-gather.11.cloned.1.call-start = ((), (), s32[]{:S(2)}) async-start(), calls=%async_computation.3 | async-start | bytes 2129920 | tf_op jit(solution)/shard_map/all_gather | solution.py:104
  11.1 7.8 collective-permute-start
  13.1 7.7 collective-permute-start.1
  20.7 7.1 copy-start.9
  21.9 35.7 %collective-permute-start.3 = (bf16[2,4,160,512]{3,2,1,0:T(8,128)(2,1)}, bf16[2,4,160,512]{3,2,1,0:T(8,128)(2,1)}, u32[]{:S(2)}, u32[]{:S(2)}) collective-permute-start(bf16[2,4,160,512]{3,2,1,0:T(8,128)(2,1)} %pad_maximum_fusion.1), channel_id=1, source_target_pairs={{16,0},{20,4},{24,8},{28,12},{32,16},{36,20},{40,24},{44,28},{48,3... | collective-permute-start | bytes 3932168 | tf_op jit(solution)/shard_map/ppermute | solution.py:30
  23.2 38.2 %collective-permute-start.2 = (bf16[2,4,160,512]{3,2,1,0:T(8,128)(2,1)}, bf16[2,4,160,512]{3,2,1,0:T(8,128)(2,1)S(1)}, u32[]{:S(2)}, u32[]{:S(2)}) collective-permute-start(bf16[2,4,160,512]{3,2,1,0:T(8,128)(2,1)} %pad_maximum_fusion.1), channel_id=1, source_target_pairs={{0,16},{4,20},{8,24},{12,28},{16,32},{20,36},{24,40},{28,44},{32,4... | collective-permute-start | bytes 3932168 | tf_op jit(solution)/shard_map/ppermute | solution.py:30
  27.8 1315.0 %all-gather.9.cloned.1.call-start = ((), (), s32[]{:S(2)}) async-start(), calls=%async_computation.2 | async-start | bytes 2129920 | tf_op jit(solution)/shard_map/all_gather | solution.py:103
  63.2 255.7 %copy-start.5 = (bf16[2,4,128,512]{3,2,1,0:T(8,128)(2,1)S(1)}, bf16[2,4,128,512]{3,2,1,0:T(8,128)(2,1)}, u32[]{:S(2)}) copy-start(bf16[2,4,128,512]{3,2,1,0:T(8,128)(2,1)} %get-tuple-element.17) | copy-start | bytes 3145732
  316.7 4.1 copy-start.2
  319.0 1.9 copy-start.8
  320.8 1.2 copy-start.7
  321.5 1.3 copy-start.6
  322.7 1.3 copy-start.3
  325.4 1.2 copy-start.4
  326.6 1.2 copy-start
  328.6 13.7 %collective-permute-start.4 = (bf16[2,4,64,512]{3,2,1,0:T(8,128)(2,1)S(1)}, bf16[2,4,64,512]{3,2,1,0:T(8,128)(2,1)S(1)}, u32[]{:S(2)}, u32[]{:S(2)}) collective-permute-start(bf16[2,4,64,512]{3,2,1,0:T(8,128)(2,1)S(1)} %get-tuple-element.23), channel_id=1, source_target_pairs={{0,1},{1,2},{2,3},{4,5},{5,6},{6,7},{8,9},{9,10},{10,11},{12,13},{... | collective-permute-start | bytes 1572872 | tf_op jit(solution)/shard_map/ppermute | solution.py:18
  330.6 13.3 collective-permute-start.5
  345.4 360.0 %collective-permute-start.7 = (bf16[2,4,256,512]{3,2,1,0:T(8,128)(2,1)}, bf16[2,4,256,512]{3,2,1,0:T(8,128)(2,1)}, u32[]{:S(2)}, u32[]{:S(2)}) collective-permute-start(bf16[2,4,256,512]{3,2,1,0:T(8,128)(2,1)} %pad_maximum_fusion), channel_id=1, source_target_pairs={{64,0},{68,4},{72,8},{76,12},{80,16},{84,20},{88,24},{92,28},{96,3... | collective-permute-start | bytes 6291464 | tf_op jit(solution)/shard_map/ppermute | solution.py:30
  346.7 362.2 %collective-permute-start.6 = (bf16[2,4,256,512]{3,2,1,0:T(8,128)(2,1)}, bf16[2,4,256,512]{3,2,1,0:T(8,128)(2,1)}, u32[]{:S(2)}, u32[]{:S(2)}) collective-permute-start(bf16[2,4,256,512]{3,2,1,0:T(8,128)(2,1)} %pad_maximum_fusion), channel_id=1, source_target_pairs={{0,64},{4,68},{8,72},{12,76},{16,80},{20,84},{24,88},{28,92},{32,9... | collective-permute-start | bytes 6291464 | tf_op jit(solution)/shard_map/ppermute | solution.py:30
  701.5 2.5 copy-start.1
Sparse Core Ops, SparseCore 0:
  9.1 307.5 all-gather.4
  318.5 382.9 all-gather.6
  703.3 340.5 all-gather.10
  1045.6 297.1 all-gather.8
where the time goes:
time: 1360 us
  waiting for transfers between devices  1270 us (93%)
  starting transfers between devices  31.3 us (2%)
  matrix products  25.5 us (2%)
    all_gather x2, waiting for transfers between devices, apply_convolution(): lax.all_gather(weight, 'rows', axis=2, tiled=True)  598 us
    all_gather x1, waiting for transfers between devices, feed_forward(): lax.all_gather(down_weight, 'rows', axis=0, tiled=True)  329 us
    all_gather x1, waiting for transfers between devices, feed_forward(): lax.all_gather(up_rows, 'rows', axis=0, tiled=True)  299 us
    ppermute x4, waiting for transfers between devices, passed_along(): return lax.ppermute(array, axis, pairs)  27.6 us
  transfers between devices with their start and end apart: 12, of which 9 were waited for; matrix products, arithmetic and copies ran while one was open for 3% of the time, Pallas kernels for 0%

commit v1 on v0

--- a/solution.py
+++ b/solution.py
@@ -82,7 +82,12 @@
     if far_reach:
         summed = add_taps(zeroed, lax.all_gather(weight, "rows", axis=2, tiled=True))
     else:
-        summed = add_taps(zeroed, lax.all_gather(weight, "rows", axis=2, tiled=True))
+        summed = add_taps(
+            zeroed,
+            jnp.concatenate(
+                lax.all_to_all(jnp.stack([weight] * lax.axis_size("rows")), "rows", 0, 0), axis=2
+            ),
+        )
     return summed.reshape(normed.shape)
 
 

time: 1360 us -> 1070 us (0.79)
  waiting for transfers between devices: 1270 us -> 963 us
  starting transfers between devices: 31.3 us -> 45.3 us
    all_gather x2 -> x1, waiting for transfers between devices: 598 us -> 141 us  [apply_convolution(): lax.all_gather(weight, 'rows', axis=2, tiled=True)]
    ppermute x4, waiting for transfers between devices: 27.6 us -> 132 us  [passed_along(): return lax.ppermute(array, axis, pairs)]
    all_gather x1, waiting for transfers between devices: 299 us -> 376 us  [feed_forward(): lax.all_gather(up_rows, 'rows', axis=0, tiled=True)]
    all_gather x1, waiting for transfers between devices: 329 us -> 299 us  [feed_forward(): lax.all_gather(down_weight, 'rows', axis=0, tiled=True)]
  transfers between devices with their start and end apart: 12 -> 12, of which waited for: 9 -> 7; matrix products, arithmetic and copies ran while one was open for 3% -> 4% of each run, Pallas kernels for 0% -> 0%
where the time goes in v1:
time: 1070 us
  waiting for transfers between devices  963 us (90%)
  starting transfers between devices  45.3 us (4%)
  matrix products  22.3 us (2%)
  local copies, waits for them, and re-layouts  20.4 us (2%)
  between operations  13.4 us (1%)
    all_gather x1, waiting for transfers between devices, feed_forward(): lax.all_gather(up_rows, 'rows', axis=0, tiled=True)  376 us
    all_gather x1, waiting for transfers between devices, feed_forward(): lax.all_gather(down_weight, 'rows', axis=0, tiled=True)  299 us
    all_gather x1, waiting for transfers between devices, apply_convolution(): lax.all_gather(weight, 'rows', axis=2, tiled=True)  141 us
    ppermute x4, waiting for transfers between devices, passed_along(): return lax.ppermute(array, axis, pairs)  132 us
  transfers between devices with their start and end apart: 12, of which 7 were waited for; matrix products, arithmetic and copies ran while one was open for 4% of the time, Pallas kernels for 0%

profile of v1, /device:TPU:16, one launch (start us, length us, event | category | flops | bytes accessed | tf_op | source)
XLA Modules:
  0.0 1073.0 jit_solution(9039446056064633297)
XLA Ops:
  7.3 3.3 stack.2
  10.5 13.0 %all-to-all-start = ((bf16[64,3,3,8,512]{4,3,2,1,0:T(8,128)(2,1)}), bf16[64,3,3,8,512]{4,3,2,1,0:T(8,128)(2,1)}, u32[]{:S(2)}, u32[]{:S(2)}) async-start(bf16[64,3,3,8,512]{4,3,2,1,0:T(8,128)(2,1)} %stack.2), calls=%async_computation | async-start | bytes 9437184 | tf_op jit(solution)/shard_map/all_to_all | solution.py:88
  24.2 1.9 collective-permute-start
  26.2 5.1 collective-permute-start.1
  31.3 7.1 collective-permute-done
  40.9 5.6 collective-permute-start.2
  47.8 131.6 %collective-permute-done.3 = bf16[2,4,160,512]{3,2,1,0:T(8,128)(2,1)} collective-permute-done((bf16[2,4,160,512]{3,2,1,0:T(8,128)(2,1)}, bf16[2,4,160,512]{3,2,1,0:T(8,128)(2,1)}, u32[]{:S(2)}, u32[]{:S(2)}) %collective-permute-start.3) | collective-permute-done | bytes 1310752 | tf_op jit(solution)/shard_map/ppermute | solution.py:30
  179.4 3.7 fusion.47
  183.1 3.6 fusion.48
  186.8 2.8 copy.8
  197.4 1.5 add_add_fusion.1
  199.8 1.9 collective-permute-start.4
  201.7 5.1 collective-permute-start.5
  206.9 6.2 collective-permute-done.4
  213.1 1.9 collective-permute-done.5
  214.9 1.5 pad_maximum_fusion
  217.8 9.9 collective-permute-start.6
  227.7 141.0 %all-gather.4.cloned.1.call-done = bf16[3,3,512,512]{3,2,1,0:T(8,128)(2,1)} async-done(((bf16[3,3,8,512]{3,2,1,0:T(8,128)(2,1)}), bf16[3,3,512,512]{3,2,1,0:T(8,128)(2,1)}) %all-gather.4.cloned.1.call-update) | async-done | bytes 4718608 | tf_op jit(solution)/shard_map/all_gather | solution.py:83
  368.7 1.9 fusion.25
  372.6 2.1 fusion.45
  376.1 2.2 fusion.46
  383.3 375.6 %all-gather.6.cloned.1.call-done = bf16[2048,512]{1,0:T(8,128)(2,1)} async-done(((bf16[32,512]{1,0:T(8,128)(2,1)}), bf16[2048,512]{1,0:T(8,128)(2,1)}) %all-gather.6.cloned.1.call-update) | async-done | bytes 2097168 | tf_op jit(solution)/shard_map/all_gather | solution.py:108
  758.9 299.0 %all-gather.8.cloned.1.call-done = bf16[2048,512]{1,0:T(8,128)(2,1)} async-done(((bf16[32,512]{1,0:T(8,128)(2,1)}), bf16[2048,512]{1,0:T(8,128)(2,1)}) %all-gather.8.cloned.1.call-update) | async-done | bytes 2097168 | tf_op jit(solution)/shard_map/all_gather | solution.py:109
  1058.0 7.2 fusion.8
  (62 shorter events, 24.6 us)
Async XLA Ops:
  6.5 362.2 %all-gather.4.cloned.1.call-start = ((), (), s32[]{:S(2)}) async-start(), calls=%async_computation.1 | async-start | bytes 4792320 | tf_op jit(solution)/shard_map/all_gather | solution.py:83
  10.5 13.1 %copy-start = (bf16[2,4,128,512]{3,2,1,0:T(8,128)(2,1)S(1)}, bf16[2,4,128,512]{3,2,1,0:T(8,128)(2,1)}, u32[]{:S(2)}) copy-start(bf16[2,4,128,512]{3,2,1,0:T(8,128)(2,1)} %param.5) | copy-start | bytes 3145732
  10.5 176.3 %all-to-all-start = ((bf16[64,3,3,8,512]{4,3,2,1,0:T(8,128)(2,1)}), bf16[64,3,3,8,512]{4,3,2,1,0:T(8,128)(2,1)}, u32[]{:S(2)}, u32[]{:S(2)}) async-start(bf16[64,3,3,8,512]{4,3,2,1,0:T(8,128)(2,1)} %stack.2), calls=%async_computation | async-start | bytes 9437184 | tf_op jit(solution)/shard_map/all_to_all | solution.py:88
  23.6 735.4 %all-gather.6.cloned.1.call-start = ((), (), s32[]{:S(2)}) async-start(), calls=%async_computation.2 | async-start | bytes 2129920 | tf_op jit(solution)/shard_map/all_gather | solution.py:108
  24.2 14.1 %collective-permute-start = (bf16[2,4,16,512]{3,2,1,0:T(8,128)(2,1)S(1)}, bf16[2,4,16,512]{3,2,1,0:T(8,128)(2,1)S(1)}, u32[]{:S(2)}, u32[]{:S(2)}) collective-permute-start(bf16[2,4,16,512]{3,2,1,0:T(8,128)(2,1)S(1)} %get-tuple-element.27), channel_id=1, source_target_pairs={{0,1},{1,2},{2,3},{4,5},{5,6},{6,7},{8,9},{9,10},{10,11},{12,13},{... | collective-permute-start | bytes 393224 | tf_op jit(solution)/shard_map/ppermute | solution.py:18
  26.2 12.2 %collective-permute-start.1 = (bf16[2,4,16,512]{3,2,1,0:T(8,128)(2,1)S(1)}, bf16[2,4,16,512]{3,2,1,0:T(8,128)(2,1)S(1)}, u32[]{:S(2)}, u32[]{:S(2)}) collective-permute-start(bf16[2,4,16,512]{3,2,1,0:T(8,128)(2,1)S(1)} %get-tuple-element.28), channel_id=1, source_target_pairs={{1,0},{2,1},{3,2},{5,4},{6,5},{7,6},{9,8},{10,9},{11,10},{13,12},{... | collective-permute-start | bytes 393224 | tf_op jit(solution)/shard_map/ppermute | solution.py:20
  39.6 139.8 %collective-permute-start.3 = (bf16[2,4,160,512]{3,2,1,0:T(8,128)(2,1)}, bf16[2,4,160,512]{3,2,1,0:T(8,128)(2,1)}, u32[]{:S(2)}, u32[]{:S(2)}) collective-permute-start(bf16[2,4,160,512]{3,2,1,0:T(8,128)(2,1)} %pad_maximum_fusion.1), channel_id=1, source_target_pairs={{16,0},{20,4},{24,8},{28,12},{32,16},{36,20},{40,24},{44,28},{48,3... | collective-permute-start | bytes 3932168 | tf_op jit(solution)/shard_map/ppermute | solution.py:30
  40.9 142.3 %collective-permute-start.2 = (bf16[2,4,160,512]{3,2,1,0:T(8,128)(2,1)}, bf16[2,4,160,512]{3,2,1,0:T(8,128)(2,1)}, u32[]{:S(2)}, u32[]{:S(2)}) collective-permute-start(bf16[2,4,160,512]{3,2,1,0:T(8,128)(2,1)} %pad_maximum_fusion.1), channel_id=1, source_target_pairs={{0,16},{4,20},{8,24},{12,28},{16,32},{20,36},{24,40},{28,44},{32,4... | collective-permute-start | bytes 3932168 | tf_op jit(solution)/shard_map/ppermute | solution.py:30
  46.5 1011.4 %all-gather.8.cloned.1.call-start = ((), (), s32[]{:S(2)}) async-start(), calls=%async_computation.3 | async-start | bytes 2129920 | tf_op jit(solution)/shard_map/all_gather | solution.py:109
  186.8 2.9 copy-start.5
  189.6 1.2 copy-start.4
  190.4 1.3 copy-start.8
  191.6 1.3 copy-start.7
  192.4 1.3 copy-start.6
  193.5 1.3 copy-start.2
  196.2 1.2 copy-start.3
  199.8 13.3 %collective-permute-start.4 = (bf16[2,4,64,512]{3,2,1,0:T(8,128)(2,1)S(1)}, bf16[2,4,64,512]{3,2,1,0:T(8,128)(2,1)S(1)}, u32[]{:S(2)}, u32[]{:S(2)}) collective-permute-start(bf16[2,4,64,512]{3,2,1,0:T(8,128)(2,1)S(1)} %get-tuple-element.23), channel_id=1, source_target_pairs={{0,1},{1,2},{2,3},{4,5},{5,6},{6,7},{8,9},{9,10},{10,11},{12,13},{... | collective-permute-start | bytes 1572872 | tf_op jit(solution)/shard_map/ppermute | solution.py:18
  201.7 13.2 %collective-permute-start.5 = (bf16[2,4,64,512]{3,2,1,0:T(8,128)(2,1)S(1)}, bf16[2,4,64,512]{3,2,1,0:T(8,128)(2,1)S(1)}, u32[]{:S(2)}, u32[]{:S(2)}) collective-permute-start(bf16[2,4,64,512]{3,2,1,0:T(8,128)(2,1)S(1)} %get-tuple-element.24), channel_id=1, source_target_pairs={{1,0},{2,1},{3,2},{5,4},{6,5},{7,6},{9,8},{10,9},{11,10},{13,12},{... | collective-permute-start | bytes 1572872 | tf_op jit(solution)/shard_map/ppermute | solution.py:20
  216.5 156.1 %collective-permute-start.7 = (bf16[2,4,256,512]{3,2,1,0:T(8,128)(2,1)}, bf16[2,4,256,512]{3,2,1,0:T(8,128)(2,1)}, u32[]{:S(2)}, u32[]{:S(2)}) collective-permute-start(bf16[2,4,256,512]{3,2,1,0:T(8,128)(2,1)} %pad_maximum_fusion), channel_id=1, source_target_pairs={{64,0},{68,4},{72,8},{76,12},{80,16},{84,20},{88,24},{92,28},{96,3... | collective-permute-start | bytes 6291464 | tf_op jit(solution)/shard_map/ppermute | solution.py:30
  217.8 158.4 %collective-permute-start.6 = (bf16[2,4,256,512]{3,2,1,0:T(8,128)(2,1)}, bf16[2,4,256,512]{3,2,1,0:T(8,128)(2,1)}, u32[]{:S(2)}, u32[]{:S(2)}) collective-permute-start(bf16[2,4,256,512]{3,2,1,0:T(8,128)(2,1)} %pad_maximum_fusion), channel_id=1, source_target_pairs={{0,64},{4,68},{8,72},{12,76},{16,80},{20,84},{24,88},{28,92},{32,9... | collective-permute-start | bytes 6291464 | tf_op jit(solution)/shard_map/ppermute | solution.py:30
  368.7 2.5 copy-start.1
Sparse Core Ops, SparseCore 0:
  9.1 359.5 all-gather.3
  370.5 388.3 all-gather.5
  760.7 297.1 all-gather.7
